TPU v7x, 32 devices: a whole 2x2x4 slice. The times are simulated.
32 devices in a mesh: tm: 8 (over y, x, core), feed: 4 (over z).
Axes of the slice: x: 2, y: 2, z: 4, core: 2. Of those that a mesh axis runs over, the one named last changes fastest.
Arguments:
- voltages: bfloat16 [1024, 16384], P('feed', 'tm'), may hold values from -6 to 6
- coefficients: float32 [16, 2048], replicated, may hold values from -1.5 to 1.5
- beam_weights: bfloat16 [1024, 1024, 2, 512], P('tm', 'feed'), may hold values from -0.1875 to 0.1875
Outputs:
- beam_power: float32 [1, 1024, 512], P(None, 'tm', 'feed')
All inputs are finite; a program needn't handle non-finite values.
Results may differ from a plain program's by a relative error of at most 0.0025.
Values may be sent and summed in bfloat16 or wider, within the bound.
A program may use at most 128 MiB of HBM per device.

v0:
```python
import math

import jax
import jax.numpy as jnp
from jax import lax
from jax.sharding import PartitionSpec as P

INTEG = 8


def shifted(value, axis, steps):
    count = lax.axis_size(axis)
    initial, last = (max(0, -steps), min(count, count - steps))
    return lax.ppermute(value, axis, [(source, source + steps) for source in range(initial, last)])


def dft_table(frame_len):
    channels = frame_len // 2
    sample = lax.broadcasted_iota(jnp.int32, (frame_len, channels), 0)
    channel = lax.broadcasted_iota(jnp.int32, (frame_len, channels), 1)
    angles = 2.0 * math.pi / frame_len * (sample * channel % frame_len).astype(jnp.float32)
    norming = 1.0 / math.sqrt(frame_len)
    stacked = jnp.stack([jnp.cos(angles) * norming, -jnp.sin(angles) * norming], axis=2)
    return stacked.reshape(frame_len, 2 * channels).astype(jnp.bfloat16)


def polyphase(extended, coefficients, frames):
    tap_count = coefficients.shape[0]
    running = jnp.zeros((extended.shape[0], frames, extended.shape[2]), jnp.float32)
    for tap_index in range(tap_count):
        running = running + coefficients[tap_index][None, None, :] * extended[
            :, tap_index : tap_index + frames, :
        ].astype(jnp.float32)
    return running.astype(jnp.bfloat16)


def sign_pairs(arranged):
    real_part = arranged[:, :, 0]
    imag_part = arranged[:, :, 1]
    for_real = jnp.stack([real_part, -imag_part], axis=2)
    for_imag = jnp.stack([imag_part, real_part], axis=2)
    return (for_real, for_imag)


def form_beams(for_real, for_imag, weight_part):
    beam_re = jnp.einsum(
        "tcrf,cfrb->bct", for_real, weight_part, preferred_element_type=jnp.float32
    )
    beam_im = jnp.einsum(
        "tcrf,cfrb->bct", for_imag, weight_part, preferred_element_type=jnp.float32
    )
    return jnp.stack([beam_re, beam_im], axis=1)


def detect(beams):
    energy = jnp.sum(beams * beams, axis=1)
    beam_count, per_group, total_frames = energy.shape
    binned = jnp.mean(energy.reshape(beam_count, per_group, total_frames // INTEG, INTEG), axis=3)
    return jnp.transpose(binned, (2, 1, 0))


def local(voltages, coefficients, beam_weights):
    feeds_here, samples = voltages.shape
    tap_count, frame_len = coefficients.shape
    look_ahead = tap_count - 1
    transform = dft_table(frame_len)
    frames = samples // frame_len
    blocks = voltages.reshape(feeds_here, frames, frame_len)
    neighbours = min((look_ahead + frames - 1) // frames, lax.axis_size("tm") - 1)
    pieces = [blocks]
    for distance in range(1, neighbours + 1):
        pieces.append(shifted(blocks, "tm", -distance))
    collected = sum((segment.shape[1] for segment in pieces))
    if collected < frames + look_ahead:
        pieces.append(
            jnp.zeros((feeds_here, frames + look_ahead - collected, frame_len), jnp.bfloat16)
        )
    extended = jnp.concatenate(pieces, axis=1)
    filtered = polyphase(extended, coefficients, frames)
    spectra = jnp.einsum(
        "ftk,kc->tcf", filtered, transform, preferred_element_type=jnp.float32
    ).astype(jnp.bfloat16)
    turned = lax.all_to_all(spectra, "tm", split_axis=1, concat_axis=0, tiled=True)
    total_frames, paired, feed_width = turned.shape
    per_group = paired // 2
    arranged = turned.reshape(total_frames, per_group, 2, feed_width)
    for_real, for_imag = sign_pairs(arranged)
    beams = lax.psum_scatter(
        form_beams(for_real, for_imag, beam_weights), "feed", scatter_dimension=0, tiled=True
    )
    return detect(beams)


def solution(mesh):
    placed = (P("feed", "tm"), P(), P("tm", "feed", None, None))
    return jax.shard_map(
        local, mesh=mesh, in_specs=placed, out_specs=P(None, "tm", "feed"), check_vma=False
    )
```

profile of v0, /device:TPU:0, one launch (start us, length us, event | category | flops | bytes accessed | tf_op | source)
XLA Modules:
  0.0 342.5 jit_solution(9087678974341301015)
XLA Ops:
  6.5 0.0 reduce-scatter.2.cloned.1.call-start
  6.5 1.3 collective-permute-start.6
  7.8 1.3 collective-permute-start.5
  9.1 1.3 collective-permute-start.4
  10.4 1.3 collective-permute-start.3
  11.7 1.3 collective-permute-start.2
  13.0 20.3 %collective-permute-done.6 = bf16[256,1,2048]{2,0,1:T(8,128)(2,1)S(1)} collective-permute-done((bf16[256,1,2048]{2,0,1:T(8,128)(2,1)}, bf16[256,1,2048]{2,0,1:T(8,128)(2,1)S(1)}, u32[]{:S(2)}, u32[]{:S(2)}) %collective-permute-start.6) | collective-permute-done | bytes 1048608 | tf_op jit(solution)/shard_map/ppermute | solution.py:14
  33.3 1.3 collective-permute-start.1
  34.6 2.4 collective-permute-done.5
  37.0 1.3 collective-permute-start
  38.3 34.9 %multiply_convert_fusion = (bf16[2048,1024,1]{1,0,2:T(8,128)(2,1)S(1)}, bf16[2048,1024,1]{1,0,2:T(8,128)(2,1)}) fusion(), kind=kLoop, calls=%fused_computation.11 | loop fusion | flops 39845888 | bytes 8388608 | tf_op jit(solution)/shard_map/convert.1
  73.2 6.2 %pad_maximum_fusion = bf16[2048,1024,2]{1,0,2:T(8,128)(2,1)} fusion(bf16[2048,1024,1]{1,0,2:T(8,128)(2,1)S(1)} %get-tuple-element.25, bf16[2048,1024,1]{1,0,2:T(8,128)(2,1)} %get-tuple-element.26), kind=kLoop, calls=%fused_computation.10 | loop fusion | flops 4194304 | bytes 16777216 | tf_op jit(solution)/shard_map/stack | solution.py:23
  79.3 21.5 %copy.20 = bf16[2048,1024,2]{0,2,1:T(2,128)(2,1)} copy(bf16[2048,1024,2]{1,0,2:T(8,128)(2,1)} %pad_maximum_fusion) | data formatting | bytes 16777216 | tf_op jit(solution)/shard_map/stack | solution.py:23
  100.8 0.0 copy-start
  100.8 0.0 copy-start.1
  100.8 13.2 %convert_element_type.70 = bf16[2048,2048]{0,1:T(8,128)(2,1)} reshape(bf16[2048,1024,2]{0,2,1:T(2,128)(2,1)} %copy.20) | data formatting | bytes 16777216 | tf_op jit(solution)/shard_map/convert_element_type | solution.py:24
  114.0 0.0 copy-done
  114.0 0.1 fusion.59
  114.1 0.0 collective-permute-done.4
  114.1 0.0 collective-permute-done.3
  114.2 0.0 collective-permute-done.2
  114.2 0.0 collective-permute-done.1
  114.2 0.0 collective-permute-done
  114.2 0.0 copy-done.1
  114.2 8.8 %fusion.10 = bf16[1,2048,256]{2,1,0:T(8,128)(2,1)S(1)} fusion(bf16[2048,2048]{0,1:T(8,128)(2,1)} %convert_element_type.70, bf16[256,1,2048]{2,0,1:T(8,128)(2,1)S(1)} %collective-permute-done.6, bf16[256,1,2048]{2,0,1:T(8,128)(2,1)S(1)} %collective-permute-done.5, bf16[256,1,2048]{2,0,1:T(8,128)(2,1)} %collective-permute-done.4, ...), kind=kOutput, calls=%fused_computation.18 | convolution fusion | flops 2164785152 | bytes 17956864 | tf_op jit(solution)/shard_map/ftk,kc->tcf/dot_general | solution.py:80
  123.0 11.7 %copy.41 = bf16[1,2048,256]{2,0,1:T(2,128)(2,1)S(1)} copy(bf16[1,2048,256]{2,1,0:T(8,128)(2,1)S(1)} %fusion.10) | data formatting | bytes 2097152 | tf_op jit(solution)/shard_map/convert_element_type | solution.py:82
  134.7 0.5 broadcast.177
  135.3 10.6 %reduce.5 = bf16[2048,256]{1,0:T(8,128)(2,1)S(1)} reduce(bf16[2048,1,256]{2,1,0:T(2,128)(2,1)S(1)} %bitcast.83, bf16[]{:T(256)} %broadcast.177), dimensions={1}, to_apply=%bitcast.82.reduce_sub_computation | reduce | bytes 2097154
  145.9 0.3 reshape.181
  146.1 37.2 %all_to_all.4 = bf16[8,2,32768]{2,1,0:T(2,128)(2,1)S(1)} all-to-all(bf16[8,2,32768]{2,1,0:T(2,128)(2,1)S(1)} %reshape.181), channel_id=1, replica_groups=mesh['tm'=8,'feed'=4] {'tm'}, dimensions={0} | all-to-all | bytes 2097152 | tf_op jit(solution)/shard_map/all_to_all | solution.py:83
  183.4 1.0 reshape.182
  184.4 11.0 %bitcast_reduce_fusion = bf16[2048,256]{1,0:T(8,128)(2,1)S(1)} fusion(bf16[2048,1,256]{2,1,0:T(2,128)(2,1)S(1)} %reshape.182), kind=kLoop, calls=%fused_computation.74 | loop fusion | bytes 2097152 | tf_op jit(solution)/shard_map/all_to_all | solution.py:83
  195.4 0.4 reshape.177
  195.9 1.5 fusion.58
  197.4 0.6 copy.29
  198.0 1.4 fusion.57
  199.4 25.6 %fusion.29 = f32[512,1,128,8]{0,3,2,1:T(8,128)S(1)} fusion(bf16[128,256,2,512]{3,2,1,0:T(2,128)(2,1)} %param.5, bf16[8,128,1,256]{3,0,2,1:T(8,128)(2,1)S(1)} %copy.29, bf16[8,128,1,256]{3,0,2,1:T(8,128)(2,1)} %get-tuple-element.6), kind=kOutput, calls=%fused_computation.36 | convolution fusion | flops 537395200 | bytes 70254592 | tf_op jit(solution)/shard_map/tcrf,cfrb->bct/dot_general | solution.py:49
  225.0 27.1 %fusion.26 = f32[512,1,128,8]{0,3,2,1:T(8,128)} fusion(bf16[128,256,2,512]{3,2,1,0:T(2,128)(2,1)} %param.5, bf16[8,128,1,256]{3,0,2,1:T(8,128)(2,1)S(1)} %get-tuple-element.5, bf16[8,128,1,256]{3,0,2,1:T(8,128)(2,1)S(1)} %copy.29), kind=kOutput, calls=%fused_computation.35 | convolution fusion | flops 537395200 | bytes 70254592 | tf_op jit(solution)/shard_map/tcrf,cfrb->bct/dot_general | solution.py:46
  252.1 4.0 %pad_maximum_fusion.1 = f32[512,2,128,8]{0,3,2,1:T(8,128)} fusion(f32[512,1,128,8]{0,3,2,1:T(8,128)S(1)} %fusion.29, f32[512,1,128,8]{0,3,2,1:T(8,128)} %fusion.26), kind=kLoop, calls=%fused_computation.16 | loop fusion | flops 1048576 | bytes 8388608 | tf_op jit(solution)/shard_map/stack | solution.py:52
  256.0 0.0 reduce-scatter.2.cloned.1.call-update
  256.0 77.6 %reduce-scatter.2.cloned.1.call-done = f32[128,2,128,8]{0,3,2,1:T(8,128)} async-done(((f32[512,2,128,8]{0,3,2,1:T(8,128)}), f32[128,2,128,8]{0,3,2,1:T(8,128)}) %reduce-scatter.2.cloned.1.call-update) | async-done | bytes 1048592 | tf_op jit(solution)/shard_map/reduce_scatter | solution.py:88
  333.6 1.4 multiply_reduce_fusion
  335.0 0.6 multiply_bitcast_fusion
Async XLA Ops:
  6.5 327.1 %reduce-scatter.2.cloned.1.call-start = ((), (), s32[]{:S(2)}) async-start(), calls=%async_computation.2 | async-start | bytes 5242880 | tf_op jit(solution)/shard_map/reduce_scatter | solution.py:88
  6.5 26.8 %collective-permute-start.6 = (bf16[256,1,2048]{2,0,1:T(8,128)(2,1)}, bf16[256,1,2048]{2,0,1:T(8,128)(2,1)S(1)}, u32[]{:S(2)}, u32[]{:S(2)}) collective-permute-start(bf16[256,1,2048]{2,0,1:T(8,128)(2,1)} %bitcast.100), channel_id=1, source_target_pairs={{28,0},{29,1},{30,2},{31,3}} | collective-permute-start | bytes 3145736 | tf_op jit(solution)/shard_map/ppermute | solution.py:14
  7.8 29.2 %collective-permute-start.5 = (bf16[256,1,2048]{2,0,1:T(8,128)(2,1)}, bf16[256,1,2048]{2,0,1:T(8,128)(2,1)S(1)}, u32[]{:S(2)}, u32[]{:S(2)}) collective-permute-start(bf16[256,1,2048]{2,0,1:T(8,128)(2,1)} %bitcast.101), channel_id=1, source_target_pairs={{24,0},{28,4},{25,1},{29,5},{26,2},{30,6},{27,3},{31,7}} | collective-permute-start | bytes 3145736 | tf_op jit(solution)/shard_map/ppermute | solution.py:14
  9.1 105.0 %collective-permute-start.4 = (bf16[256,1,2048]{2,0,1:T(8,128)(2,1)}, bf16[256,1,2048]{2,0,1:T(8,128)(2,1)}, u32[]{:S(2)}, u32[]{:S(2)}) collective-permute-start(bf16[256,1,2048]{2,0,1:T(8,128)(2,1)} %bitcast.102), channel_id=1, source_target_pairs={{20,0},{24,4},{28,8},{21,1},{25,5},{29,9},{22,2},{26,6},{30,10},{2... | collective-permute-start | bytes 3145736 | tf_op jit(solution)/shard_map/ppermute | solution.py:14
  10.4 103.7 %collective-permute-start.3 = (bf16[256,1,2048]{2,0,1:T(8,128)(2,1)}, bf16[256,1,2048]{2,0,1:T(8,128)(2,1)}, u32[]{:S(2)}, u32[]{:S(2)}) collective-permute-start(bf16[256,1,2048]{2,0,1:T(8,128)(2,1)} %bitcast.103), channel_id=1, source_target_pairs={{16,0},{20,4},{24,8},{28,12},{17,1},{21,5},{25,9},{29,13},{18,2},{... | collective-permute-start | bytes 3145736 | tf_op jit(solution)/shard_map/ppermute | solution.py:14
  11.7 102.4 %collective-permute-start.2 = (bf16[256,1,2048]{2,0,1:T(8,128)(2,1)}, bf16[256,1,2048]{2,0,1:T(8,128)(2,1)}, u32[]{:S(2)}, u32[]{:S(2)}) collective-permute-start(bf16[256,1,2048]{2,0,1:T(8,128)(2,1)} %bitcast.104), channel_id=1, source_target_pairs={{12,0},{16,4},{20,8},{24,12},{28,16},{13,1},{17,5},{21,9},{25,13},... | collective-permute-start | bytes 3145736 | tf_op jit(solution)/shard_map/ppermute | solution.py:14
  33.3 80.9 %collective-permute-start.1 = (bf16[256,1,2048]{2,0,1:T(8,128)(2,1)}, bf16[256,1,2048]{2,0,1:T(8,128)(2,1)}, u32[]{:S(2)}, u32[]{:S(2)}) collective-permute-start(bf16[256,1,2048]{2,0,1:T(8,128)(2,1)} %bitcast.105), channel_id=1, source_target_pairs={{8,0},{12,4},{16,8},{20,12},{24,16},{28,20},{9,1},{13,5},{17,9},{2... | collective-permute-start | bytes 3145736 | tf_op jit(solution)/shard_map/ppermute | solution.py:14
  37.0 77.2 %collective-permute-start = (bf16[256,1,2048]{2,0,1:T(8,128)(2,1)}, bf16[256,1,2048]{2,0,1:T(8,128)(2,1)}, u32[]{:S(2)}, u32[]{:S(2)}) collective-permute-start(bf16[256,1,2048]{2,0,1:T(8,128)(2,1)} %bitcast.106), channel_id=1, source_target_pairs={{4,0},{8,4},{12,8},{16,12},{20,16},{24,20},{28,24},{5,1},{9,5},{13... | collective-permute-start | bytes 3145736 | tf_op jit(solution)/shard_map/ppermute | solution.py:14
  100.8 13.2 %copy-start = (f32[16,2048]{1,0:T(8,128)S(1)}, f32[16,2048]{1,0:T(8,128)}, u32[]{:S(2)}) copy-start(f32[16,2048]{1,0:T(8,128)} %param.4) | copy-start | bytes 393220
  100.8 13.4 %copy-start.1 = (bf16[256,2048]{1,0:T(8,128)(2,1)S(1)}, bf16[256,2048]{1,0:T(8,128)(2,1)}, u32[]{:S(2)}) copy-start(bf16[256,2048]{1,0:T(8,128)(2,1)} %param.3) | copy-start | bytes 3145732
Sparse Core Ops, SparseCore 0:
  256.2 77.4 reduce-scatter.1
where the time goes:
time: 344 us; the launch traced here: 343 us
  waiting for transfers between devices  100 us (29%)
  local copies, waits for them, and re-layouts  61.8 us (18%)
  matrix products  61.5 us (18%)
  other arithmetic  59.1 us (17%)
  blocking collectives  37.2 us (11%)
  between operations  13.6 us (4%)
  starting transfers between devices  9.01 us (3%)
    reduce_scatter x1, waiting for transfers between devices, local(): lax.psum_scatter(form_beams(for_real, for_imag, beam_weights), 'feed', sc...  77.6 us
    all_to_all x1, blocking collectives, local(): lax.all_to_all(spectra, 'tm', split_axis=1, concat_axis=0, tiled=True)  37.2 us
    another operation x1, other arithmetic  34.9 us
    dot_general x1, matrix products, form_beams(): jnp.einsum('tcrf,cfrb->bct', for_real, weight_part, preferred_element_typ...  27.1 us
    dot_general x1, matrix products, form_beams(): jnp.einsum('tcrf,cfrb->bct', for_imag, weight_part, preferred_element_typ...  25.6 us
    ppermute x7, waiting for transfers between devices, shifted(): lax.ppermute(value, axis, [(source, source + steps) for source in range(i...  22.7 us
    another operation x1, local copies, waits for them, and re-layouts, dft_table(): jnp.stack([jnp.cos(angles) * norming, -jnp.sin(angles) * norming], axis=2)  21.5 us
    convert_element_type x1, local copies, waits for them, and re-layouts, dft_table(): return stacked.reshape(frame_len, 2 * channels).astype(jnp.bfloat16)  13.2 us
  transfers between devices with their start and end apart: 8, of which 3 were waited for; matrix products, arithmetic and copies ran while one was open for 22% of the time, Pallas kernels for 0%

commit v1 on v0

--- a/solution.py
+++ b/solution.py
@@ -1,8 +1,13 @@
+import functools
 import math
 
 import jax
 import jax.numpy as jnp
+import ml_dtypes
+import numpy as np
 from jax import lax
+from jax.experimental import pallas as pl
+from jax.experimental.pallas import tpu as pltpu
 from jax.sharding import PartitionSpec as P
 
 INTEG = 8
@@ -59,7 +64,7 @@
     return jnp.transpose(binned, (2, 1, 0))
 
 
-def local(voltages, coefficients, beam_weights):
+def general(voltages, coefficients, beam_weights):
     feeds_here, samples = voltages.shape
     tap_count, frame_len = coefficients.shape
     look_ahead = tap_count - 1
@@ -91,6 +96,236 @@
     return detect(beams)
 
 
+def grouped_table(frame_len, groups):
+    channels = frame_len // 2
+    remainder = (np.arange(frame_len)[:, None] * np.arange(channels)[None, :]) % frame_len
+    angles = 2.0 * math.pi / frame_len * remainder
+    parts = np.stack([np.cos(angles), -np.sin(angles)], axis=1) / math.sqrt(frame_len)
+    split = parts.reshape(frame_len, 2, groups, channels // groups)
+    arranged = split.transpose(2, 0, 1, 3).reshape(groups, frame_len, 2 * channels // groups)
+    return np.ascontiguousarray(arranged).astype(ml_dtypes.bfloat16)
+
+
+def greet(axis, n):
+    me = lax.axis_index(axis)
+    barrier = pltpu.get_barrier_semaphore()
+    for k in range(1, n):
+        pl.semaphore_signal(
+            barrier, inc=1, device_id={axis: lax.rem(me + k, n)}, device_id_type=pl.DeviceIdType.MESH
+        )
+    pl.semaphore_wait(barrier, n - 1)
+
+
+def channelize_kernel(
+    n, volt, coef, table, out, frames, held, filt, staged, landed,
+    table_sem, send1, recv1, send2, recv2,
+):
+    me = lax.axis_index("tm")
+    rows = frames.shape[1]
+    taps, frame_len = coef.shape
+    fetch = pltpu.make_async_copy(table, held, table_sem)
+    fetch.start()
+    greet("tm", n)
+
+    def first(k, source):
+        dest = lax.rem(me + k, n)
+        return pltpu.make_async_remote_copy(
+            src_ref=volt.at[pl.ds(pl.multiple_of(dest * rows, rows), rows)],
+            dst_ref=frames.at[source],
+            send_sem=send1.at[k],
+            recv_sem=recv1.at[source],
+            device_id={"tm": dest},
+            device_id_type=pl.DeviceIdType.MESH,
+        )
+
+    for k in range(1, n):
+        first(k, me).start()
+    frames[me] = volt[pl.ds(pl.multiple_of(me * rows, rows), rows), :]
+    for k in range(1, n):
+        first(k, lax.rem(me + n - k, n)).wait_recv()
+
+    width = 128
+
+    def columns(step, carry):
+        cols = pl.ds(pl.multiple_of(step * width, width), width)
+        samples = [frames[t, :, cols].astype(jnp.float32) for t in range(n)]
+        for t in range(n):
+            running = coef[0:1, cols] * samples[t]
+            for p in range(1, min(taps, n - t)):
+                running = running + coef[p : p + 1, cols] * samples[t + p]
+            filt[t * rows : (t + 1) * rows, cols] = running.astype(jnp.bfloat16)
+        return carry
+
+    lax.fori_loop(0, frame_len // width, columns, 0)
+    fetch.wait()
+
+    def second(k, source):
+        return pltpu.make_async_remote_copy(
+            src_ref=staged.at[k],
+            dst_ref=landed.at[source],
+            send_sem=send2.at[k],
+            recv_sem=recv2.at[source],
+            device_id={"tm": lax.rem(me + k, n)},
+            device_id_type=pl.DeviceIdType.MESH,
+        )
+
+    def transform(group):
+        return jnp.dot(filt[...], held[group], preferred_element_type=jnp.float32).astype(jnp.bfloat16)
+
+    def send(k, carry):
+        staged[k] = transform(lax.rem(me + k, n))
+        second(k, me).start()
+        return carry
+
+    lax.fori_loop(1, n, send, 0)
+    landed[me] = transform(me)
+    for k in range(1, n):
+        second(k, lax.rem(me + n - k, n)).wait_recv()
+    for k in range(1, n):
+        first(k, me).wait_send()
+        second(k, me).wait_send()
+    out[...] = landed[...]
+
+
+def channelize(voltages, coefficients, n):
+    feeds_here, frame_len = voltages.shape
+    rows = feeds_here // n
+    paired = frame_len // n
+    vmem = pl.BlockSpec(memory_space=pltpu.VMEM)
+    dma = pltpu.SemaphoreType.DMA
+    return pl.pallas_call(
+        functools.partial(channelize_kernel, n),
+        out_shape=jax.ShapeDtypeStruct((n, n * rows, paired), jnp.bfloat16),
+        in_specs=[vmem, vmem, pl.BlockSpec(memory_space=pl.ANY)],
+        out_specs=vmem,
+        scratch_shapes=[
+            pltpu.VMEM((n, rows, frame_len), jnp.bfloat16),
+            pltpu.VMEM((n, frame_len, paired), jnp.bfloat16),
+            pltpu.VMEM((n * rows, frame_len), jnp.bfloat16),
+            pltpu.VMEM((n, n * rows, paired), jnp.bfloat16),
+            pltpu.VMEM((n, n * rows, paired), jnp.bfloat16),
+            dma, dma((n,)), dma((n,)), dma((n,)), dma((n,)),
+        ],
+        compiler_params=pltpu.CompilerParams(
+            collective_id=0, has_side_effects=True, vmem_limit_bytes=40 << 20
+        ),
+    )(voltages, coefficients, grouped_table(frame_len, n))
+
+
+def beams_kernel(n, left, weights, out, formed, own, staged, landed, send_sem, recv_sem):
+    step = pl.program_id(0)
+    steps = pl.num_programs(0)
+    me = lax.axis_index("feed")
+    group, feeds_here, _, beams = weights.shape
+    share = beams // n
+
+    def copy(k, at):
+        block = pl.ds(pl.multiple_of(at * group, group), group)
+        return pltpu.make_async_remote_copy(
+            src_ref=staged.at[k - 1, block],
+            dst_ref=landed.at[k - 1, block],
+            send_sem=send_sem.at[k - 1, at],
+            recv_sem=recv_sem.at[k - 1, at],
+            device_id={"feed": lax.rem(me + k, n)},
+            device_id_type=pl.DeviceIdType.MESH,
+        )
+
+    @pl.when(step == 0)
+    def _():
+        greet("feed", n)
+
+    def one(c, carry):
+        weight = weights.at[c].reshape(2 * feeds_here, beams)[...]
+        formed[c] = jnp.dot(left[c], weight, preferred_element_type=jnp.float32)
+        return carry
+
+    lax.fori_loop(0, group, one, 0, unroll=4)
+    here = pl.ds(pl.multiple_of(step * group, group), group)
+    for k in range(n - 1, 0, -1):
+        dest = lax.rem(me + k, n)
+        staged[k - 1, here] = formed[
+            :, :, pl.ds(pl.multiple_of(dest * share, share), share)
+        ].astype(jnp.bfloat16)
+        copy(k, step).start()
+    own[here] = formed[:, :, pl.ds(pl.multiple_of(me * share, share), share)]
+
+    @pl.when(step == steps - 1)
+    def _():
+        def finish(at, carry):
+            block = pl.ds(pl.multiple_of(at * group, group), group)
+            total = own[block]
+            for k in range(1, n):
+                copy(k, at).wait()
+                total = total + landed[k - 1, block].astype(jnp.float32)
+            out[block] = jnp.sum(total * total, axis=1) * (1.0 / INTEG)
+            return carry
+
+        lax.fori_loop(0, steps, finish, 0)
+
+
+def beams_power(left, weights, n):
+    channels, rows, depth = left.shape
+    feeds_here, beams = weights.shape[1], weights.shape[3]
+    share = beams // n
+    group = 8
+    steps = channels // group
+    dma = pltpu.SemaphoreType.DMA
+    return pl.pallas_call(
+        functools.partial(beams_kernel, n),
+        grid=(steps,),
+        out_shape=jax.ShapeDtypeStruct((channels, share), jnp.float32),
+        in_specs=[
+            pl.BlockSpec((group, rows, depth), lambda i: (i, 0, 0)),
+            pl.BlockSpec((group, feeds_here, 2, beams), lambda i: (i, 0, 0, 0)),
+        ],
+        out_specs=pl.BlockSpec((channels, share), lambda i: (0, 0)),
+        scratch_shapes=[
+            pltpu.VMEM((group, rows, beams), jnp.float32),
+            pltpu.VMEM((channels, rows, share), jnp.float32),
+            pltpu.VMEM((n - 1, channels, rows, share), jnp.bfloat16),
+            pltpu.VMEM((n - 1, channels, rows, share), jnp.bfloat16),
+            dma((n - 1, steps)), dma((n - 1, steps)),
+        ],
+        compiler_params=pltpu.CompilerParams(
+            collective_id=1, has_side_effects=True, vmem_limit_bytes=40 << 20
+        ),
+    )(left, weights)
+
+
+def left_operand(turned, total_frames):
+    n, _, paired = turned.shape
+    split = turned.reshape(n, total_frames, -1, 2, paired // 2)
+    real, imag = split[:, :, :, 0], split[:, :, :, 1]
+    pairs = jnp.stack([jnp.stack([real, -imag]), jnp.stack([imag, real])])
+    arranged = jnp.transpose(pairs, (5, 0, 3, 2, 4, 1))
+    return arranged.reshape(paired // 2, 2 * total_frames, -1)
+
+
+def fast(voltages, coefficients, beam_weights):
+    n_tm, n_feed = lax.axis_size("tm"), lax.axis_size("feed")
+    turned = channelize(voltages, coefficients, n_tm)
+    left = left_operand(turned, n_tm)
+    return beams_power(left, beam_weights, n_feed)[None]
+
+
+def fits(voltages, coefficients, beam_weights):
+    n_tm, n_feed = lax.axis_size("tm"), lax.axis_size("feed")
+    feeds_here, samples = voltages.shape
+    frame_len = coefficients.shape[1]
+    return (
+        samples == frame_len
+        and n_tm == INTEG
+        and feeds_here % (16 * n_tm) == 0
+        and frame_len % (256 * n_tm) == 0
+        and beam_weights.shape[3] % (128 * n_feed) == 0
+    )
+
+
+def local(voltages, coefficients, beam_weights):
+    plan = fast if fits(voltages, coefficients, beam_weights) else general
+    return plan(voltages, coefficients, beam_weights)
+
+
 def solution(mesh):
     placed = (P("feed", "tm"), P(), P("tm", "feed", None, None))
     return jax.shard_map(

time: 344 us -> 100 us (0.29)
  waiting for transfers between devices: 100 us -> 0 us
  Pallas kernels: 0 us -> 84.4 us
  matrix products: 61.5 us -> 0 us
  other arithmetic: 59.1 us -> 0.52 us
  local copies, waits for them, and re-layouts: 61.8 us -> 14.9 us
  blocking collectives: 37.2 us -> 0 us
  between operations: 13.6 us -> 0.07 us
  starting transfers between devices: 9.01 us -> 0 us
    pallas_call x0 -> x2, Pallas kernels: none -> 84.4 us  [the longest x1 54.2 us: beams_power(): pl.pallas_call(functools.partial(beams_kernel, n), grid=(steps,), out_sha...]
    reduce_scatter x1 -> x0, waiting for transfers between devices: 77.6 us -> none  [local(): lax.psum_scatter(form_beams(for_real, for_imag, beam_weights), 'feed', sc...]
    dot_general x3 -> x0, matrix products: 61.5 us -> none  [the longest x1 27.1 us: form_beams(): jnp.einsum('tcrf,cfrb->bct', for_real, weight_part, preferred_element_typ...]
    another operation x3 -> x1, other arithmetic: 45 us -> 0.18 us  [left_operand(): pairs = jnp.stack([jnp.stack([real, -imag]), jnp.stack([imag, real])])]
    all_to_all x1 -> x0, blocking collectives: 37.2 us -> none  [local(): lax.all_to_all(spectra, 'tm', split_axis=1, concat_axis=0, tiled=True)]
    convert_element_type x2 -> x0, local copies, waits for them, and re-layouts: 25 us -> none  [the longest x1 13.2 us: dft_table(): return stacked.reshape(frame_len, 2 * channels).astype(jnp.bfloat16)]
    ppermute x7 -> x0, waiting for transfers between devices: 22.7 us -> none  [shifted(): lax.ppermute(value, axis, [(source, source + steps) for source in range(i...]
    another operation x1 -> x0, local copies, waits for them, and re-layouts: 21.5 us -> none  [dft_table(): jnp.stack([jnp.cos(angles) * norming, -jnp.sin(angles) * norming], axis=2)]
  transfers between devices with their start and end apart: 8 -> 0, of which waited for: 3 -> 0; matrix products, arithmetic and copies ran while one was open for 22% -> 0% of each run, Pallas kernels for 0% -> 0%
where the time goes in v1:
time: 100 us; the launch traced here: 99.9 us
  Pallas kernels  84.4 us (84%)
  local copies, waits for them, and re-layouts  14.9 us (15%)
    pallas_call x1, Pallas kernels, beams_power(): pl.pallas_call(functools.partial(beams_kernel, n), grid=(steps,), out_sha...  54.2 us
    pallas_call x1, Pallas kernels, channelize(): pl.pallas_call(functools.partial(channelize_kernel, n), out_shape=jax.Sha...  30.2 us
    unnamed x8, local copies, waits for them, and re-layouts  6.23 us
    reshape x1, local copies, waits for them, and re-layouts, left_operand(): return arranged.reshape(paired // 2, 2 * total_frames, -1)  3.92 us
    slice x1, local copies, waits for them, and re-layouts, left_operand(): real, imag = (split[:, :, :, 0], split[:, :, :, 1])  2.29 us
    transpose x1, local copies, waits for them, and re-layouts, left_operand(): arranged = jnp.transpose(pairs, (5, 0, 3, 2, 4, 1))  2.16 us

profile of v1, /device:TPU:0, one launch (start us, length us, event | category | flops | bytes accessed | tf_op | source)
XLA Modules:
  0.0 99.9 jit_solution(8067921396960574880)
XLA Ops:
  0.0 0.0 copy-start
  0.0 3.4 %copy-done = bf16[8,2048,256]{2,1,0:T(8,128)(2,1)S(1)} copy-done((bf16[8,2048,256]{2,1,0:T(8,128)(2,1)S(1)}, bf16[8,2048,256]{2,1,0:T(8,128)(2,1)}, u32[]{:S(2)}) %copy-start) | copy-done | bytes 8388632
  3.4 0.0 copy-start.1
  3.4 1.2 %copy-done.1 = bf16[256,2048]{1,0:T(8,128)(2,1)S(1)} copy-done((bf16[256,2048]{1,0:T(8,128)(2,1)S(1)}, bf16[256,2048]{1,0:T(8,128)(2,1)}, u32[]{:S(2)}) %copy-start.1) | copy-done | bytes 1048600
  4.6 0.0 copy-start.2
  4.6 0.9 copy-done.2
  5.5 30.2 %shard_map.46 = bf16[8,256,256]{2,1,0:T(8,128)(2,1)S(1)} custom-call(bf16[256,2048]{1,0:T(8,128)(2,1)S(1)} %copy-done.1, f32[16,2048]{1,0:T(8,128)S(1)} %copy-done.2, bf16[8,2048,256]{2,1,0:T(8,128)(2,1)S(1)} %copy-done), custom_call_target="tpu_custom_call" | custom-call | tf_op jit(solution)/shard_map/pallas_call | solution.py:196
  35.7 0.3 reshape.16
  36.0 2.3 %fusion.1 = (bf16[8,8,32,1,128]{4,3,2,1,0:T(2,128)(2,1)S(1)}, bf16[8,8,32,1,128]{4,3,2,1,0:T(2,128)(2,1)S(1)}) fusion(bf16[8,8,32,2,128]{4,3,2,1,0:T(2,128)(2,1)S(1)} %reshape.16), kind=kLoop, calls=%fused_computation.6 | loop fusion | bytes 2097152 | tf_op jit(solution)/shard_map/slice | solution.py:298
  38.3 0.1 fusion
  38.4 0.1 copy.17
  38.5 0.2 maximum_bitcast_fusion.1
  38.7 0.2 maximum_bitcast_fusion
  38.9 2.2 %copy.10 = bf16[128,2,8,8,32,2]{0,2,1,5,4,3:T(8,128)(2,1)} copy(bf16[128,2,8,8,32,2]{0,4,2,3,5,1:T(8,128)(2,1)S(1)} %maximum_bitcast_fusion) | data formatting | bytes 4194304 | tf_op jit(solution)/shard_map/transpose | solution.py:300
  41.1 3.9 %copy.11.left = bf16[128,16,512]{2,1,0:T(8,128)(2,1)S(1)} copy(bf16[128,16,512]{0,1,2:T(8,128)(2,1)} %bitcast.15) | data formatting | bytes 4194304 | tf_op jit(solution)/shard_map/reshape | solution.py:301
  45.0 54.2 %shard_map.47 = f32[128,128]{1,0:T(8,128)S(1)} custom-call(bf16[128,16,512]{2,1,0:T(8,128)(2,1)S(1)} %copy.11.left, bf16[128,256,2,512]{3,2,1,0:T(2,128)(2,1)} %weights.1), custom_call_target="tpu_custom_call" | custom-call | tf_op jit(solution)/shard_map/pallas_call | solution.py:273
  99.3 0.6 copy.19
Async XLA Ops:
  0.0 3.4 %copy-start = (bf16[8,2048,256]{2,1,0:T(8,128)(2,1)S(1)}, bf16[8,2048,256]{2,1,0:T(8,128)(2,1)}, u32[]{:S(2)}) copy-start(bf16[8,2048,256]{2,1,0:T(8,128)(2,1)} %constant.2.clone.table) | copy-start | bytes 25165828
  3.4 1.2 %copy-start.1 = (bf16[256,2048]{1,0:T(8,128)(2,1)S(1)}, bf16[256,2048]{1,0:T(8,128)(2,1)}, u32[]{:S(2)}) copy-start(bf16[256,2048]{1,0:T(8,128)(2,1)} %volt.1) | copy-start | bytes 3145732
  4.6 0.9 copy-start.2

commit v2 on v1

--- a/solution.py
+++ b/solution.py
@@ -103,7 +103,7 @@
     parts = np.stack([np.cos(angles), -np.sin(angles)], axis=1) / math.sqrt(frame_len)
     split = parts.reshape(frame_len, 2, groups, channels // groups)
     arranged = split.transpose(2, 0, 1, 3).reshape(groups, frame_len, 2 * channels // groups)
-    return np.ascontiguousarray(arranged).astype(ml_dtypes.bfloat16)
+    return arranged.astype(ml_dtypes.bfloat16).astype(np.float32)
 
 
 def greet(axis, n):
@@ -117,14 +117,16 @@
 
 
 def channelize_kernel(
-    n, volt, coef, table, out, frames, held, filt, staged, landed,
-    table_sem, send1, recv1, send2, recv2,
+    n, volt, taps_in, table, out, frames, wide, held, filt, staged, landed, coef,
+    table_sem, coef_sem, own_sem, send1, recv1, send2, recv2,
 ):
     me = lax.axis_index("tm")
     rows = frames.shape[1]
     taps, frame_len = coef.shape
-    fetch = pltpu.make_async_copy(table, held, table_sem)
-    fetch.start()
+    fetch = pltpu.make_async_copy(table, wide, table_sem)
+    taps_copy = pltpu.make_async_copy(taps_in, coef, coef_sem)
+    own_rows = pl.ds(pl.multiple_of(me * rows, rows), rows)
+    own_copy = pltpu.make_async_copy(volt.at[own_rows], frames.at[me], own_sem)
     greet("tm", n)
 
     def first(k, source):
@@ -140,10 +142,24 @@
 
     for k in range(1, n):
         first(k, me).start()
-    frames[me] = volt[pl.ds(pl.multiple_of(me * rows, rows), rows), :]
+    own_copy.start()
+    taps_copy.start()
+    fetch.start()
+    fetch.wait()
+    chunk = 128
+    per = frame_len // chunk
+
+    def narrow(step, carry):
+        part = pl.ds(pl.multiple_of(lax.rem(step, per) * chunk, chunk), chunk)
+        held[step // per, part] = wide[step // per, part].astype(jnp.bfloat16)
+        return carry
+
+    lax.fori_loop(0, n * per, narrow, 0)
     for k in range(1, n):
         first(k, lax.rem(me + n - k, n)).wait_recv()
 
+    own_copy.wait()
+    taps_copy.wait()
     width = 128
 
     def columns(step, carry):
@@ -157,7 +173,6 @@
         return carry
 
     lax.fori_loop(0, frame_len // width, columns, 0)
-    fetch.wait()
 
     def second(k, source):
         return pltpu.make_async_remote_copy(
@@ -196,68 +211,131 @@
     return pl.pallas_call(
         functools.partial(channelize_kernel, n),
         out_shape=jax.ShapeDtypeStruct((n, n * rows, paired), jnp.bfloat16),
-        in_specs=[vmem, vmem, pl.BlockSpec(memory_space=pl.ANY)],
+        in_specs=[pl.BlockSpec(memory_space=pl.ANY)] * 3,
         out_specs=vmem,
         scratch_shapes=[
             pltpu.VMEM((n, rows, frame_len), jnp.bfloat16),
+            pltpu.VMEM((n, frame_len, paired), jnp.float32),
             pltpu.VMEM((n, frame_len, paired), jnp.bfloat16),
             pltpu.VMEM((n * rows, frame_len), jnp.bfloat16),
             pltpu.VMEM((n, n * rows, paired), jnp.bfloat16),
             pltpu.VMEM((n, n * rows, paired), jnp.bfloat16),
-            dma, dma((n,)), dma((n,)), dma((n,)), dma((n,)),
+            pltpu.VMEM(coefficients.shape, jnp.float32),
+            dma, dma, dma, dma((n,)), dma((n,)), dma((n,)), dma((n,)),
         ],
         compiler_params=pltpu.CompilerParams(
-            collective_id=0, has_side_effects=True, vmem_limit_bytes=40 << 20
+            collective_id=0, has_side_effects=True, vmem_limit_bytes=60 << 20
         ),
     )(voltages, coefficients, grouped_table(frame_len, n))
 
 
-def beams_kernel(n, left, weights, out, formed, own, staged, landed, send_sem, recv_sem):
+def beams_kernel(n, left, weights, out, formed, staged, ahead, behind, send_sem, ahead_sem, behind_sem):
     step = pl.program_id(0)
     steps = pl.num_programs(0)
     me = lax.axis_index("feed")
     group, feeds_here, _, beams = weights.shape
     share = beams // n
 
-    def copy(k, at):
-        block = pl.ds(pl.multiple_of(at * group, group), group)
+    def block(at):
+        return pl.ds(pl.multiple_of(at * group, group), group)
+
+    def copy(dest, at, up):
         return pltpu.make_async_remote_copy(
-            src_ref=staged.at[k - 1, block],
-            dst_ref=landed.at[k - 1, block],
-            send_sem=send_sem.at[k - 1, at],
-            recv_sem=recv_sem.at[k - 1, at],
-            device_id={"feed": lax.rem(me + k, n)},
+            src_ref=staged.at[dest, block(at)],
+            dst_ref=(ahead if up else behind).at[dest, block(at)],
+            send_sem=send_sem.at[dest, at],
+            recv_sem=(ahead_sem if up else behind_sem).at[dest, at],
+            device_id={"feed": jnp.minimum(me + 1, n - 1) if up else jnp.maximum(me - 1, 0)},
             device_id_type=pl.DeviceIdType.MESH,
         )
 
+    def mine(dest, at):
+        return formed[block(at), :, dest * share : (dest + 1) * share]
+
     @pl.when(step == 0)
     def _():
-        greet("feed", n)
+        barrier = pltpu.get_barrier_semaphore()
+        for k in range(1, n):
+            pl.semaphore_signal(
+                barrier, inc=1, device_id={"feed": lax.rem(me + k, n)}, device_id_type=pl.DeviceIdType.MESH
+            )
+        pl.semaphore_wait(barrier, n - 1)
 
     def one(c, carry):
         weight = weights.at[c].reshape(2 * feeds_here, beams)[...]
-        formed[c] = jnp.dot(left[c], weight, preferred_element_type=jnp.float32)
+        formed[step * group + c] = jnp.dot(left[c], weight, preferred_element_type=jnp.float32)
         return carry
 
     lax.fori_loop(0, group, one, 0, unroll=4)
-    here = pl.ds(pl.multiple_of(step * group, group), group)
-    for k in range(n - 1, 0, -1):
-        dest = lax.rem(me + k, n)
-        staged[k - 1, here] = formed[
-            :, :, pl.ds(pl.multiple_of(dest * share, share), share)
-        ].astype(jnp.bfloat16)
-        copy(k, step).start()
-    own[here] = formed[:, :, pl.ds(pl.multiple_of(me * share, share), share)]
+
+    def begin(dest, at, up):
+        staged[dest, block(at)] = mine(dest, at).astype(jnp.bfloat16)
+        copy(dest, at, up).start()
+
+    def relay(dest, at, up):
+        copy(dest, at, up).wait_recv()
+        landed = (ahead if up else behind)[dest, block(at)].astype(jnp.float32)
+        staged[dest, block(at)] = (mine(dest, at) + landed).astype(jnp.bfloat16)
+        copy(dest, at, up).start()
+
+    @pl.when(me == 0)
+    def _():
+        for dest in range(n - 1, 0, -1):
+            begin(dest, step, True)
+
+    @pl.when(me == n - 1)
+    def _():
+        for dest in range(n - 1):
+            begin(dest, step, False)
+
+    def pass_on(at):
+        for dest in range(n - 1, 1, -1):
+            @pl.when((me > 0) & (dest > me))
+            def _():
+                relay(dest, at, True)
+
+        for dest in range(n - 2):
+            @pl.when((me < n - 1) & (dest < me))
+            def _():
+                relay(dest, at, False)
+
+    lag = 2
+
+    @pl.when(step >= lag)
+    def _():
+        pass_on(step - lag)
 
     @pl.when(step == steps - 1)
     def _():
+        for back in range(lag, 0, -1):
+            pass_on(steps - back)
+
         def finish(at, carry):
-            block = pl.ds(pl.multiple_of(at * group, group), group)
-            total = own[block]
-            for k in range(1, n):
-                copy(k, at).wait()
-                total = total + landed[k - 1, block].astype(jnp.float32)
-            out[block] = jnp.sum(total * total, axis=1) * (1.0 / INTEG)
+            for dest in range(n):
+                @pl.when(dest < me)
+                def _():
+                    copy(dest, at, False).wait_send()
+
+                @pl.when(dest > me)
+                def _():
+                    copy(dest, at, True).wait_send()
+
+                @pl.when(dest == me)
+                def _():
+                    formed[block(at), :, :share] = mine(dest, at)
+
+            @pl.when(me > 0)
+            def _():
+                copy(me, at, True).wait_recv()
+                formed[block(at), :, :share] = formed[block(at), :, :share] + ahead[me, block(at)].astype(jnp.float32)
+
+            @pl.when(me < n - 1)
+            def _():
+                copy(me, at, False).wait_recv()
+                formed[block(at), :, :share] = formed[block(at), :, :share] + behind[me, block(at)].astype(jnp.float32)
+
+            total = formed[block(at), :, :share]
+            out[block(at)] = jnp.sum(total * total, axis=1) * (1.0 / INTEG)
             return carry
 
         lax.fori_loop(0, steps, finish, 0)
@@ -270,6 +348,7 @@
     group = 8
     steps = channels // group
     dma = pltpu.SemaphoreType.DMA
+    slots = pltpu.VMEM((n, channels, rows, share), jnp.bfloat16)
     return pl.pallas_call(
         functools.partial(beams_kernel, n),
         grid=(steps,),
@@ -280,11 +359,9 @@
         ],
         out_specs=pl.BlockSpec((channels, share), lambda i: (0, 0)),
         scratch_shapes=[
-            pltpu.VMEM((group, rows, beams), jnp.float32),
-            pltpu.VMEM((channels, rows, share), jnp.float32),
-            pltpu.VMEM((n - 1, channels, rows, share), jnp.bfloat16),
-            pltpu.VMEM((n - 1, channels, rows, share), jnp.bfloat16),
-            dma((n - 1, steps)), dma((n - 1, steps)),
+            pltpu.VMEM((channels, rows, beams), jnp.float32),
+            slots, slots, slots,
+            dma((n, steps)), dma((n, steps)), dma((n, steps)),
         ],
         compiler_params=pltpu.CompilerParams(
             collective_id=1, has_side_effects=True, vmem_limit_bytes=40 << 20

time: 100 us -> 162 us (1.62)
  Pallas kernels: 84.4 us -> 151 us
  local copies, waits for them, and re-layouts: 14.9 us -> 10.4 us
    pallas_call x1, Pallas kernels: 54.2 us -> 120 us  [beams_power(): pl.pallas_call(functools.partial(beams_kernel, n), grid=(steps,), out_sha...]
    unnamed x8 -> x2, local copies, waits for them, and re-layouts: 6.23 us -> 0.72 us
where the time goes in v2:
time: 162 us
  Pallas kernels  151 us (93%)
  local copies, waits for them, and re-layouts  10.4 us (6%)
    pallas_call x1, Pallas kernels, beams_power(): pl.pallas_call(functools.partial(beams_kernel, n), grid=(steps,), out_sha...  120 us
    pallas_call x1, Pallas kernels, channelize(): pl.pallas_call(functools.partial(channelize_kernel, n), out_shape=jax.Sha...  30.8 us
    reshape x1, local copies, waits for them, and re-layouts, left_operand(): return arranged.reshape(paired // 2, 2 * total_frames, -1)  3.92 us

profile of v2, /device:TPU:0, one launch (start us, length us, event | category | flops | bytes accessed | tf_op | source)
XLA Modules:
  0.0 161.9 jit_solution(10287604952903565346)
XLA Ops:
  0.0 30.8 %shard_map.46 = bf16[8,256,256]{2,1,0:T(8,128)(2,1)} custom-call(bf16[256,2048]{1,0:T(8,128)(2,1)} %volt.1, f32[16,2048]{1,0:T(8,128)} %taps_in.1, f32[8,2048,256]{2,1,0:T(8,128)} %constant.2.clone.table), custom_call_target="tpu_custom_call" | custom-call | tf_op jit(solution)/shard_map/pallas_call | solution.py:211
  30.8 1.3 reshape.16
  32.1 2.3 %fusion.1 = (bf16[8,8,32,1,128]{4,3,2,1,0:T(2,128)(2,1)S(1)}, bf16[8,8,32,1,128]{4,3,2,1,0:T(2,128)(2,1)S(1)}) fusion(bf16[8,8,32,2,128]{4,3,2,1,0:T(2,128)(2,1)S(1)} %reshape.16), kind=kLoop, calls=%fused_computation.6 | loop fusion | bytes 2097152 | tf_op jit(solution)/shard_map/slice | solution.py:375
  34.4 0.1 fusion
  34.6 0.1 copy.17
  34.7 0.2 maximum_bitcast_fusion.1
  34.9 0.2 maximum_bitcast_fusion
  35.1 2.2 %copy.10 = bf16[128,2,8,8,32,2]{0,2,1,5,4,3:T(8,128)(2,1)} copy(bf16[128,2,8,8,32,2]{0,4,2,3,5,1:T(8,128)(2,1)S(1)} %maximum_bitcast_fusion) | data formatting | bytes 4194304 | tf_op jit(solution)/shard_map/transpose | solution.py:377
  37.2 3.9 %copy.11.left = bf16[128,16,512]{2,1,0:T(8,128)(2,1)S(1)} copy(bf16[128,16,512]{0,1,2:T(8,128)(2,1)} %bitcast.15) | data formatting | bytes 4194304 | tf_op jit(solution)/shard_map/reshape | solution.py:378
  41.1 120.1 %shard_map.47 = f32[128,128]{1,0:T(8,128)S(1)} custom-call(bf16[128,16,512]{2,1,0:T(8,128)(2,1)S(1)} %copy.11.left, bf16[128,256,2,512]{3,2,1,0:T(2,128)(2,1)} %weights.1), custom_call_target="tpu_custom_call" | custom-call | tf_op jit(solution)/shard_map/pallas_call | solution.py:352
  161.3 0.6 copy.19

commit v3 on v1

--- a/solution.py
+++ b/solution.py
@@ -103,7 +103,7 @@
     parts = np.stack([np.cos(angles), -np.sin(angles)], axis=1) / math.sqrt(frame_len)
     split = parts.reshape(frame_len, 2, groups, channels // groups)
     arranged = split.transpose(2, 0, 1, 3).reshape(groups, frame_len, 2 * channels // groups)
-    return np.ascontiguousarray(arranged).astype(ml_dtypes.bfloat16)
+    return arranged.astype(ml_dtypes.bfloat16).astype(np.float32)
 
 
 def greet(axis, n):
@@ -117,14 +117,16 @@
 
 
 def channelize_kernel(
-    n, volt, coef, table, out, frames, held, filt, staged, landed,
-    table_sem, send1, recv1, send2, recv2,
+    n, volt, taps_in, table, out, frames, wide, held, filt, staged, landed, coef,
+    table_sem, coef_sem, own_sem, send1, recv1, send2, recv2,
 ):
     me = lax.axis_index("tm")
     rows = frames.shape[1]
     taps, frame_len = coef.shape
-    fetch = pltpu.make_async_copy(table, held, table_sem)
-    fetch.start()
+    fetch = pltpu.make_async_copy(table, wide, table_sem)
+    taps_copy = pltpu.make_async_copy(taps_in, coef, coef_sem)
+    own_rows = pl.ds(pl.multiple_of(me * rows, rows), rows)
+    own_copy = pltpu.make_async_copy(volt.at[own_rows], frames.at[me], own_sem)
     greet("tm", n)
 
     def first(k, source):
@@ -140,10 +142,24 @@
 
     for k in range(1, n):
         first(k, me).start()
-    frames[me] = volt[pl.ds(pl.multiple_of(me * rows, rows), rows), :]
+    own_copy.start()
+    taps_copy.start()
+    fetch.start()
+    fetch.wait()
+    chunk = 128
+    per = frame_len // chunk
+
+    def narrow(step, carry):
+        part = pl.ds(pl.multiple_of(lax.rem(step, per) * chunk, chunk), chunk)
+        held[step // per, part] = wide[step // per, part].astype(jnp.bfloat16)
+        return carry
+
+    lax.fori_loop(0, n * per, narrow, 0)
     for k in range(1, n):
         first(k, lax.rem(me + n - k, n)).wait_recv()
 
+    own_copy.wait()
+    taps_copy.wait()
     width = 128
 
     def columns(step, carry):
@@ -157,7 +173,6 @@
         return carry
 
     lax.fori_loop(0, frame_len // width, columns, 0)
-    fetch.wait()
 
     def second(k, source):
         return pltpu.make_async_remote_copy(
@@ -196,18 +211,20 @@
     return pl.pallas_call(
         functools.partial(channelize_kernel, n),
         out_shape=jax.ShapeDtypeStruct((n, n * rows, paired), jnp.bfloat16),
-        in_specs=[vmem, vmem, pl.BlockSpec(memory_space=pl.ANY)],
+        in_specs=[pl.BlockSpec(memory_space=pl.ANY)] * 3,
         out_specs=vmem,
         scratch_shapes=[
             pltpu.VMEM((n, rows, frame_len), jnp.bfloat16),
+            pltpu.VMEM((n, frame_len, paired), jnp.float32),
             pltpu.VMEM((n, frame_len, paired), jnp.bfloat16),
             pltpu.VMEM((n * rows, frame_len), jnp.bfloat16),
             pltpu.VMEM((n, n * rows, paired), jnp.bfloat16),
             pltpu.VMEM((n, n * rows, paired), jnp.bfloat16),
-            dma, dma((n,)), dma((n,)), dma((n,)), dma((n,)),
+            pltpu.VMEM(coefficients.shape, jnp.float32),
+            dma, dma, dma, dma((n,)), dma((n,)), dma((n,)), dma((n,)),
         ],
         compiler_params=pltpu.CompilerParams(
-            collective_id=0, has_side_effects=True, vmem_limit_bytes=40 << 20
+            collective_id=0, has_side_effects=True, vmem_limit_bytes=60 << 20
         ),
     )(voltages, coefficients, grouped_table(frame_len, n))
 

time: 100 us -> 96.5 us (0.965)
  local copies, waits for them, and re-layouts: 14.9 us -> 10.4 us
    unnamed x8 -> x2, local copies, waits for them, and re-layouts: 6.23 us -> 0.72 us
    reshape x1, local copies, waits for them, and re-layouts: 0.29 us -> 1.35 us  [left_operand(): split = turned.reshape(n, total_frames, -1, 2, paired // 2)]
where the time goes in v3:
time: 96.5 us; the launch traced here: 96 us
  Pallas kernels  85 us (88%)
  local copies, waits for them, and re-layouts  10.4 us (11%)
    pallas_call x1, Pallas kernels, beams_power(): pl.pallas_call(functools.partial(beams_kernel, n), grid=(steps,), out_sha...  54.2 us
    pallas_call x1, Pallas kernels, channelize(): pl.pallas_call(functools.partial(channelize_kernel, n), out_shape=jax.Sha...  30.8 us
    reshape x1, local copies, waits for them, and re-layouts, left_operand(): return arranged.reshape(paired // 2, 2 * total_frames, -1)  3.92 us
    slice x1, local copies, waits for them, and re-layouts, left_operand(): real, imag = (split[:, :, :, 0], split[:, :, :, 1])  2.29 us
    transpose x1, local copies, waits for them, and re-layouts, left_operand(): arranged = jnp.transpose(pairs, (5, 0, 3, 2, 4, 1))  2.15 us

profile of v3, /device:TPU:0, one launch (start us, length us, event | category | flops | bytes accessed | tf_op | source)
XLA Modules:
  0.0 96.0 jit_solution(5733788438991491846)
XLA Ops:
  0.0 30.8 %shard_map.46 = bf16[8,256,256]{2,1,0:T(8,128)(2,1)} custom-call(bf16[256,2048]{1,0:T(8,128)(2,1)} %volt.1, f32[16,2048]{1,0:T(8,128)} %taps_in.1, f32[8,2048,256]{2,1,0:T(8,128)} %constant.2.clone.table), custom_call_target="tpu_custom_call" | custom-call | tf_op jit(solution)/shard_map/pallas_call | solution.py:211
  30.8 1.3 %reshape.16 = bf16[8,8,32,2,128]{4,3,2,1,0:T(2,128)(2,1)S(1)} reshape(bf16[8,256,256]{2,1,0:T(8,128)(2,1)} %shard_map.46) | data formatting | bytes 2097152 | tf_op jit(solution)/shard_map/reshape | solution.py:314
  32.1 2.3 %fusion.1 = (bf16[8,8,32,1,128]{4,3,2,1,0:T(2,128)(2,1)S(1)}, bf16[8,8,32,1,128]{4,3,2,1,0:T(2,128)(2,1)S(1)}) fusion(bf16[8,8,32,2,128]{4,3,2,1,0:T(2,128)(2,1)S(1)} %reshape.16), kind=kLoop, calls=%fused_computation.6 | loop fusion | bytes 2097152 | tf_op jit(solution)/shard_map/slice | solution.py:315
  34.4 0.1 fusion
  34.6 0.1 copy.17
  34.7 0.2 maximum_bitcast_fusion.1
  34.9 0.2 maximum_bitcast_fusion
  35.1 2.2 %copy.10 = bf16[128,2,8,8,32,2]{0,2,1,5,4,3:T(8,128)(2,1)} copy(bf16[128,2,8,8,32,2]{0,4,2,3,5,1:T(8,128)(2,1)S(1)} %maximum_bitcast_fusion) | data formatting | bytes 4194304 | tf_op jit(solution)/shard_map/transpose | solution.py:317
  37.2 3.9 %copy.11.left = bf16[128,16,512]{2,1,0:T(8,128)(2,1)S(1)} copy(bf16[128,16,512]{0,1,2:T(8,128)(2,1)} %bitcast.15) | data formatting | bytes 4194304 | tf_op jit(solution)/shard_map/reshape | solution.py:318
  41.1 54.2 %shard_map.47 = f32[128,128]{1,0:T(8,128)S(1)} custom-call(bf16[128,16,512]{2,1,0:T(8,128)(2,1)S(1)} %copy.11.left, bf16[128,256,2,512]{3,2,1,0:T(2,128)(2,1)} %weights.1), custom_call_target="tpu_custom_call" | custom-call | tf_op jit(solution)/shard_map/pallas_call | solution.py:290
  95.4 0.6 copy.19
